TPU v7x, 256 devices: a whole 4x4x8 slice. The times are simulated.
256 devices in a mesh: dom: 64 (over y, x, z_hi, core), row: 4 (over z_lo).
Axes of the slice: x: 4, y: 4, z: 8 (z_hi: 2, z_lo: 4; z = z_hi * 4 + z_lo), core: 2. Of those that a mesh axis runs over, the one named last changes fastest.
Arguments:
- state: float32 [3, 64, 64, 4096], P(None, 'dom', 'row'), may hold values from -1.5 to 3, as said below
- rain: float32 [64, 64, 4096], P('dom', 'row'), may hold values from 0 to 0.5
- ground: float32 [64, 4096], P('row'), may hold values from 0 to 1
- counts: int32 [64], replicated, may hold values from 0 to 16, as said below
- slot_map: int32 [64], replicated, may hold values from 0 to 63, each once
Outputs:
- resampled: float32 [3, 64, 64, 4096], P(None, 'dom', 'row')
Inputs may be any that keep to these rules, and one draw needn't show every extreme that they name: `state`: depth (component 0) lies in 0.5 to 3; both momenta (components 1 and 2) lie in -1.5 to 1.5. counts sum to 64; one particle gets exactly 16 copies, others at most 2, many none. `slot_map`: each slot appears once.
All inputs are finite; a program needn't handle non-finite values.
Results may differ from a plain program's by a relative error of at most 0.00002.
Values sent between devices are 32-bit elements; how exact they have to be, the bound alone decides.
No kernel may reach another device: no remote copies, remote signals or barrier semaphores. Data moves between devices by JAX's collectives and lax.ppermute only.
A program may use at most 192 MiB of HBM per device.

v0:
```python
import functools

import jax
import jax.numpy as jnp
from jax import lax
from jax.experimental import pallas as pl
from jax.experimental.pallas import tpu as pltpu
from jax.sharding import Mesh, PartitionSpec as P

gravity = 9.81
courant = 0.04
LANES = 128
SUBLANES = 8


def cell_terms(depth, norm, tang):
    vel = norm / depth
    cel = jnp.sqrt(gravity * depth)
    press = 0.5 * gravity * depth * depth
    return depth, norm, tang, norm * vel + press, tang * vel, vel - cel, vel + cel


def interface(left, right):
    depth_l, norm_l, tang_l, fnorm_l, ftang_l, slow_l, fast_l = left
    depth_r, norm_r, tang_r, fnorm_r, ftang_r, slow_r, fast_r = right
    lower = jnp.minimum(jnp.minimum(slow_l, slow_r), 0.0)
    upper = jnp.maximum(jnp.maximum(fast_l, fast_r), 0.0)
    scale = 1.0 / (upper - lower)
    both = upper * lower
    return (
        (upper * norm_l - lower * norm_r + both * (depth_r - depth_l)) * scale,
        (upper * fnorm_l - lower * fnorm_r + both * (norm_r - norm_l)) * scale,
        (upper * ftang_l - lower * ftang_r + both * (tang_r - tang_l)) * scale,
    )


def both_ways(depth, flow_a, flow_b):
    inverse = 1.0 / depth
    cel = jnp.sqrt(gravity * depth)
    press = (0.5 * gravity) * depth * depth
    vel_a = flow_a * inverse
    vel_b = flow_b * inverse
    cross = flow_a * vel_b
    by_row = (depth, flow_a, flow_b, flow_a * vel_a + press, cross, vel_a - cel, vel_a + cel)
    by_col = (depth, flow_b, flow_a, flow_b * vel_b + press, cross, vel_b - cel, vel_b + cel)
    return by_row, by_col


def pack_kernel(state_ref, ground_ref, first_ref, last_ref, sems):
    rows = ground_ref.shape[0]
    copies = []
    for side, (row, out_ref) in enumerate(((rows - 1, last_ref), (0, first_ref))):
        at = pl.ds(row, 1)
        for part in range(3):
            copies.append(pltpu.make_async_copy(state_ref.at[part, 0, at], out_ref.at[part], sems.at[side, part]))
        copies.append(pltpu.make_async_copy(ground_ref.at[at], out_ref.at[3], sems.at[side, 3]))
    for copy in copies:
        copy.start()
    for copy in copies:
        copy.wait()


def write_plan(zh, counts, slots, plan_ref, level_ref, sizes):
    total = counts.shape[1]
    square = (total, total)
    i = lax.broadcasted_iota(jnp.int32, square, 0)
    j = lax.broadcasted_iota(jnp.int32, square, 1)

    def over_lanes(values):
        return jnp.sum(values, axis=1, keepdims=True)

    def over_rows(values):
        return jnp.sum(values, axis=0, keepdims=True)

    def half(places):
        return jnp.bitwise_and(jnp.right_shift(places, 1), 1)

    def place(places):
        return 2 * jnp.right_shift(places, 2) + jnp.bitwise_and(places, 1)

    cumul = over_lanes(jnp.where(j <= i, counts, 0))
    ordered = over_rows((cumul <= j).astype(jnp.int32))
    ancestor = over_lanes(jnp.where(slots == i, ordered, 0))
    crossing = jnp.logical_and(ancestor == j, half(i) != half(j))
    needed = (over_rows(crossing.astype(jnp.int32)) > 0).astype(jnp.int32)
    needed_col = over_lanes(jnp.where(i == j, needed, 0))
    earlier = jnp.logical_and(i < j, half(i) == half(j))
    rank = over_rows(jnp.where(earlier, needed_col, 0))
    rank_col = over_lanes(jnp.where(i == j, rank, 0))
    mine = jnp.logical_and(half(i) == zh, jnp.logical_and(needed_col > 0, rank_col == j))
    plan_ref[0:1, :] = over_rows(jnp.where(mine, place(i), 0))
    rank_of = over_lanes(jnp.where(ancestor == j, rank, 0))
    source = jnp.where(half(ancestor) == zh, place(ancestor), total // 2 + rank_of)
    here = jnp.logical_and(half(i) == zh, place(i) == j)
    plan_ref[1:2, :] = over_rows(jnp.where(here, source, 0))
    lower = jnp.sum(jnp.where(half(j[0:1]) == 0, needed, 0))
    most = jnp.maximum(lower, jnp.sum(needed) - lower)
    level_ref[0] = sum((most > size).astype(jnp.int32) for size in sizes[:-1])


def step_kernel(
    zh_ref, state_ref, ground_ref, rain_hbm, counts_hbm, slots_hbm,
    out_ref, plan_smem, level_ref, rain_ref, counts_ref, slots_ref, plan_ref, sems, *, unroll, tail, sizes
):
    rows, width = ground_ref.shape
    copies = [
        pltpu.make_async_copy(counts_hbm, counts_ref, sems.at[0]),
        pltpu.make_async_copy(slots_hbm, slots_ref, sems.at[1]),
        pltpu.make_async_copy(rain_hbm, rain_ref, sems.at[2]),
    ]
    for copy in copies:
        copy.start()
    tiles = width // LANES
    shape = (rows, LANES)
    lane = lax.broadcasted_iota(jnp.int32, shape, 1)
    row = lax.broadcasted_iota(jnp.int32, shape, 0)
    first_lane, last_lane = lane == 0, lane == LANES - 1
    first_row, last_row = row == 0, row == rows - 1

    def columns(tile):
        start = tile * LANES
        return pl.ds(start if isinstance(tile, int) else pl.multiple_of(start, LANES), LANES)

    def load(tile):
        at = columns(tile)
        return state_ref[0, 0, :, at], state_ref[1, 0, :, at], state_ref[2, 0, :, at], ground_ref[:, at]

    def rolled(terms):
        return tuple(pltpu.roll(term, LANES - 1, 1) for term in terms)

    def mirrored(terms):
        depth, norm, tang, fnorm, ftang, slow, fast = terms
        return depth, -norm, tang, fnorm, -ftang, -fast, -slow

    def one(tile, carry, last=False):
        by_row, by_col, bed, cells_r, bed_r, flux_before, bed_before = carry
        depth, flow_a, flow_b = by_row[:3]
        if last:
            n_row, n_col, n_bed = by_row, by_col, bed
            n_rolled, n_bed_r = mirrored(by_col), bed
        else:
            n_depth, n_a, n_b, n_bed = load(tile + 1)
            n_row, n_col = both_ways(n_depth, n_a, n_b)
            n_rolled = rolled(n_col)
            n_bed_r = pltpu.roll(n_bed, LANES - 1, 1)
        right = tuple(jnp.where(last_lane, n, c) for n, c in zip(n_rolled, cells_r))
        bed_next = jnp.where(last_lane, n_bed_r, bed_r)
        flux = interface(by_col, right)
        flux_r = tuple(pltpu.roll(f, 1, 1) for f in flux)
        flux_left = tuple(jnp.where(first_lane, b, f) for b, f in zip(flux_before, flux_r))
        bed_rolled = pltpu.roll(bed, 1, 1)
        bed_left = jnp.where(first_lane, bed_before, bed_rolled)

        above = tuple(pltpu.roll(term, 1, 0) for term in by_row)
        inner = interface(above, by_row)
        inner = tuple(jnp.where(first_row, 0.0, f) for f in inner)
        below = tuple(pltpu.roll(f, rows - 1, 0) for f in inner)
        bed_up = jnp.where(first_row, 0.0, pltpu.roll(bed, 1, 0))
        bed_down = jnp.where(last_row, 0.0, pltpu.roll(bed, rows - 1, 0))

        pull = (0.5 * courant * gravity) * depth
        new_depth = depth - courant * ((below[0] - inner[0]) + (flux[0] - flux_left[0]))
        new_a = flow_a - courant * ((below[1] - inner[1]) + (flux[2] - flux_left[2])) - pull * (bed_down - bed_up)
        new_b = flow_b - courant * ((below[2] - inner[2]) + (flux[1] - flux_left[1])) - pull * (bed_next - bed_left)
        for part, value in enumerate((new_depth, new_a, new_b)):
            for top in range(rows // SUBLANES):
                out_ref[tile, top, part] = value[top * SUBLANES : (top + 1) * SUBLANES]
        return n_row, n_col, n_bed, n_rolled, n_bed_r, flux_r, bed_rolled

    depth, flow_a, flow_b, bed = load(0)
    by_row, by_col = both_ways(depth, flow_a, flow_b)
    edge = interface(mirrored(by_col), by_col)
    carry = (by_row, by_col, bed, rolled(by_col), pltpu.roll(bed, LANES - 1, 1), edge, bed)
    steps = (tiles - max(1, min(tail, tiles))) // unroll

    def some(i, carry):
        for k in range(unroll):
            carry = one(i * unroll + k, carry)
        return carry

    carry = lax.fori_loop(0, steps, some, carry)
    for copy in copies:
        copy.wait()
    write_plan(zh_ref[0], counts_ref[...], slots_ref[...], plan_ref, level_ref, sizes)
    to_scalars = pltpu.make_async_copy(plan_ref, plan_smem, sems.at[3])
    to_scalars.start()
    for tile in range(steps * unroll, tiles):
        carry = one(tile, carry, tile == tiles - 1)
    for tile in range(tiles):
        for top in range(rows // SUBLANES):
            at = slice(top * SUBLANES, (top + 1) * SUBLANES)
            out_ref[tile, top, 0] += rain_ref[0, at, columns(tile)]
    to_scalars.wait()


def edge_kernel(strip_ref, first_ref, last_ref, top_ref, low_ref, part_ref, out_ref, top_sc, low_sc, *, strips):
    strip = strip_ref[0]

    def fluxes(inside, outside, at_wall, upward):
        own = tuple(inside[i] for i in range(4))
        far = tuple(outside[i] for i in range(4))
        depth = jnp.where(at_wall, own[0], far[0])
        norm = jnp.where(at_wall, -own[1], far[1])
        tang = jnp.where(at_wall, own[2], far[2])
        bed = jnp.where(at_wall, own[3], far[3])
        mine = cell_terms(*own[:3])
        other = cell_terms(depth, norm, tang)
        flux = interface(other, mine) if upward else interface(mine, other)
        sign = courant if upward else -courant
        pull = (0.5 * courant * gravity) * own[0] * bed
        return (
            sign * flux[0],
            sign * flux[1] + (pull if upward else -pull),
            sign * flux[2],
        )

    for part, value in enumerate(fluxes(first_ref, top_ref, strip == 0, True)):
        top_sc[part] = value
    for part, value in enumerate(fluxes(last_ref, low_ref, strip == strips - 1, False)):
        low_sc[part] = value
    tiles = out_ref.shape[0]
    tops = out_ref.shape[1]
    out_ref[...] = part_ref[...]
    for tile in range(tiles):
        for part in range(3):
            out_ref[tile, 0, part, 0:1, :] = part_ref[tile, 0, part, 0:1, :] + top_sc[part, tile : tile + 1, :]
            out_ref[tile, tops - 1, part, SUBLANES - 1 : SUBLANES, :] = (
                part_ref[tile, tops - 1, part, SUBLANES - 1 : SUBLANES, :] + low_sc[part, tile : tile + 1, :]
            )


def outgoing_kernel(plan_ref, held_ref, out_ref):
    for k in range(out_ref.shape[0]):
        out_ref[k] = held_ref[plan_ref[0, k]]


def slots_kernel(plan_ref, held_ref, crossed_ref, out_ref):
    held, most = held_ref.shape[0], crossed_ref.shape[0]
    for slot in range(out_ref.shape[0]):
        code = plan_ref[1, slot]
        near = held_ref[jnp.minimum(code, held - 1)]
        far = crossed_ref[jnp.clip(code - held, 0, most - 1)]
        out_ref[slot] = jnp.where(code < held, near, far)


def place_kernel(tiles_ref, out_hbm, rows_ref, sems):
    tiles, tops, parts = tiles_ref.shape[:3]
    copies = []
    for part in range(parts):
        for top in range(tops):
            at = pl.ds(top * SUBLANES, SUBLANES)
            for tile in range(tiles):
                rows_ref[part, at, tile * LANES : (tile + 1) * LANES] = tiles_ref[tile, top, part]
            copies.append(
                pltpu.make_async_copy(rows_ref.at[part, at], out_hbm.at[part, 0, at], sems.at[part, top])
            )
            copies[-1].start()
    for copy in copies:
        copy.wait()


def whole(count):
    return [pl.BlockSpec(memory_space=pltpu.VMEM)] * count


def params(moved):
    return dict(
        compiler_params=pltpu.CompilerParams(vmem_limit_bytes=16 * 1024 * 1024),
        cost_estimate=pl.CostEstimate(flops=moved * 40, bytes_accessed=moved, transcendentals=0),
    )


COLUMN = ("zh", "row")
UNROLL = 8
TAIL = 16
HBM = pl.BlockSpec(memory_space=pltpu.HBM)
SMEM = pl.BlockSpec(memory_space=pltpu.SMEM)


def packed_edges(state, ground):
    rows, width = ground.shape
    shape = pltpu.VMEM((4, 1, width), jnp.float32)
    return pl.pallas_call(
        pack_kernel,
        out_shape=(shape, shape),
        in_specs=[HBM, HBM],
        out_specs=whole(2),
        scratch_shapes=[pltpu.SemaphoreType.DMA((2, 4))],
        name="pack",
        **params(1 << 18),
    )(*in_hbm(state, ground))


def in_hbm(*arrays):
    return [pltpu.with_memory_space_constraint(array, pltpu.HBM) for array in arrays]


def partial_step(zh, state, rain, ground, counts, slot_map, sizes, unroll=UNROLL, tail=TAIL):
    rows, width = ground.shape
    tiles, tops = width // LANES, rows // SUBLANES
    row = (1, counts.shape[0])
    return pl.pallas_call(
        functools.partial(step_kernel, unroll=unroll, tail=tail, sizes=sizes),
        out_shape=(
            jax.ShapeDtypeStruct((tiles, tops, 3, SUBLANES, LANES), jnp.float32),
            pltpu.SMEM((2, row[1]), jnp.int32),
            pltpu.SMEM((1,), jnp.int32),
        ),
        in_specs=[SMEM] + whole(2) + [HBM] * 3,
        out_specs=whole(1) + [SMEM] * 2,
        scratch_shapes=[
            pltpu.VMEM(rain.shape, jnp.float32),
            pltpu.VMEM(row, jnp.int32),
            pltpu.VMEM(row, jnp.int32),
            pltpu.VMEM((2, row[1]), jnp.int32),
            pltpu.SemaphoreType.DMA((4,)),
        ],
        name="step",
        **params(8 << 20),
    )(zh, state, ground, *in_hbm(rain, counts.reshape(row), slot_map.reshape(row)))


def stepped_tiles(zh, state, rain, ground, counts, slot_map, sizes):
    rows, width = ground.shape
    tiles = width // LANES
    strips = lax.axis_size("row")
    first, last = packed_edges(state, ground)
    count = lax.axis_size(COLUMN)
    forward = [(i, (i + 1) % count) for i in range(count)]
    backward = [(target, source) for source, target in forward]
    top = lax.ppermute(last, COLUMN, forward)
    low = lax.ppermute(first, COLUMN, backward)
    partial, plan, level = partial_step(zh, state, rain, ground, counts, slot_map, sizes)
    strip = lax.axis_index("row").astype(jnp.int32).reshape(1)
    square = (4, tiles, LANES)
    block = pl.pallas_call(
        functools.partial(edge_kernel, strips=strips),
        out_shape=pltpu.VMEM(partial.shape, jnp.float32),
        in_specs=[SMEM] + whole(5),
        out_specs=whole(1)[0],
        scratch_shapes=[pltpu.VMEM((3, tiles, LANES), jnp.float32)] * 2,
        name="edges",
        **params(1 << 20),
    )(strip, first.reshape(square), last.reshape(square), top.reshape(square), low.reshape(square), partial)
    return block, plan, level


SWAP = [(0, 1), (1, 0)]


def blocks_for_slots(plan, block, most):
    held = lax.all_to_all(block, PLANE, split_axis=0, concat_axis=0, tiled=True)
    outgoing = pl.pallas_call(
        outgoing_kernel,
        out_shape=jax.ShapeDtypeStruct((most,) + held.shape[1:], jnp.float32),
        in_specs=[SMEM] + whole(1),
        out_specs=whole(1)[0],
        name="outgoing",
        **params(1 << 20),
    )(plan, held)
    crossed = lax.ppermute(outgoing, "zh", SWAP)
    return pl.pallas_call(
        slots_kernel,
        out_shape=jax.ShapeDtypeStruct(held.shape, jnp.float32),
        in_specs=[SMEM] + whole(2),
        out_specs=whole(1)[0],
        name="slots",
        **params(2 << 20),
    )(plan, held, crossed)


def placed_strip(block, rows, width):
    return pl.pallas_call(
        place_kernel,
        out_shape=jax.ShapeDtypeStruct((3, 1, rows, width), jnp.float32),
        in_specs=whole(1),
        out_specs=HBM,
        scratch_shapes=[
            pltpu.VMEM((3, rows, width), jnp.float32),
            pltpu.SemaphoreType.DMA((3, rows // SUBLANES)),
        ],
        name="place",
        **params(2 << 20),
    )(block)


PLANE = ("y", "x", "core")
SIZES = (8, 9, 10, 11, 12, 13, 14, 15, 16, 17, 18, 20, 24, 32)


def on_device(state, rain, ground, counts, slot_map):
    rows, width = ground.shape
    zh = lax.axis_index("zh").astype(jnp.int32).reshape(1)
    block, plan, level = stepped_tiles(zh, state, rain, ground, counts, slot_map, SIZES)
    shape = block.shape
    outgoing = block.reshape((lax.axis_size(PLANE), -1) + shape[2:])
    chosen = lax.switch(level[0], [functools.partial(blocks_for_slots, most=size) for size in SIZES], plan, outgoing)
    returned = lax.all_to_all(chosen, PLANE, split_axis=0, concat_axis=0, tiled=True)
    return placed_strip(returned.reshape(shape), rows, width)


def solution(mesh):
    fine = Mesh(mesh.devices.reshape(4, 4, 2, 2, 4), ("y", "x", "zh", "core", "row"))
    dom = ("y", "x", "zh", "core")
    placed = (P(None, dom, "row", None), P(dom, "row", None), P("row", None), P(), P())
    return jax.shard_map(
        on_device,
        mesh=fine,
        in_specs=placed,
        out_specs=P(None, dom, "row", None),
        check_vma=False,
    )
```

profile of v0, /device:TPU:1, one launch (start us, length us, event | category | flops | bytes accessed | tf_op | source)
XLA Modules:
  0.0 73.5 jit_solution(16141701105757439897)
XLA Ops:
  0.0 0.0 copy-start.1
  0.0 0.0 copy-start
  0.0 1.0 %pack.1 = (f32[4,1,4096]{2,1,0:T(1,128)S(1)}, f32[4,1,4096]{2,1,0:T(1,128)S(1)}) custom-call(f32[3,1,16,4096]{3,2,1,0:T(8,128)} %state_ref.3, f32[16,4096]{1,0:T(8,128)} %ground_ref.3), custom_call_target="tpu_custom_call" | custom-call | flops 10485760 | bytes 262144 | tf_op jit(solution)/shard_map/pack/pallas_call | solution.py:283
  1.0 6.5 %collective-permute-start.15 = (f32[4,1,4096]{2,1,0:T(1,128)S(1)}, f32[4,1,4096]{2,1,0:T(1,128)S(1)}, u32[]{:S(2)}, u32[]{:S(2)}) collective-permute-start(f32[4,1,4096]{2,1,0:T(1,128)S(1)} %get-tuple-element.110), channel_id=1, source_target_pairs={{1,0},{2,1},{3,2},{8,3},{9,8},{10,9},{11,10},{0,11},{5,4},{6,5},{7... | collective-permute-start | bytes 196616 | tf_op jit(solution)/shard_map/ppermute | solution.py:332
  7.5 0.0 collective-permute-start.14
  7.5 0.0 copy-done.1
  7.5 0.0 copy-done
  7.5 2.5 %step.1 = (f32[32,2,3,8,128]{4,3,2,1,0:T(8,128)S(1)}, s32[2,64]{1,0:T(2,128)S(4)}, s32[1]{0:T(128)S(4)}) custom-call(s32[1]{0:T(128)} %bitcast.zh_ref, f32[3,1,16,4096]{3,2,1,0:T(8,128)S(1)} %copy-done, f32[16,4096]{1,0:T(8,128)S(1)} %copy-done.1, f32[1,16,4096]{2,1,0:T(8,128)} %rain_hbm.1, s32[1,64]{1,0:T(1,128)} %bitcast.13, s32[1,64]{1,0:T(1,128)} %bitcast.14), custom_call_target="tpu_custom_call" | custom-call | flops 335544320 | bytes 8388608 | tf_op jit(solution)/shard_map/step/pallas_call | solution.py:302
  10.0 0.0 collective-permute-done.15
  10.0 1.8 %collective-permute-done.14 = f32[4,1,4096]{2,1,0:T(1,128)S(1)} collective-permute-done((f32[4,1,4096]{2,1,0:T(1,128)S(1)}, f32[4,1,4096]{2,1,0:T(1,128)S(1)}, u32[]{:S(2)}, u32[]{:S(2)}) %collective-permute-start.14) | collective-permute-done | bytes 65568 | tf_op jit(solution)/shard_map/ppermute | solution.py:331
  11.8 0.2 edges.1
  12.0 42.4 %conditional.1 = (f32[32,2,3,8,128]{4,3,2,1,0:T(8,128)S(1)}) conditional(s32[]{:T(128)} %bitcast.3, (f32[32,2,3,8,128]{4,3,2,1,0:T(8,128)S(1)}, s32[2,64]{1,0:T(2,128)S(4)}) %tuple.47, (f32[32,2,3,8,128]{4,3,2,1,0:T(8,128)S(1)}, s32[2,64]{1,0:T(2,128)S(4)}) %tuple.47, (f32[32,2,3,8,128]{4,3,2,1,0:T(8,128)S(1)}, ...), branch_computations={%region_0.0_spmd, %region_1.0_spmd, %region_2.0_spmd, %region_3.0_... | conditional | flops 125829120 | bytes 7864368 | solution.py:397
  12.1 23.2 %all_to_all.65.held_ref = f32[32,2,3,8,128]{4,3,2,1,0:T(8,128)S(1)} all-to-all(f32[32,2,3,8,128]{4,3,2,1,0:T(8,128)S(1)} %get-tuple-element.80), channel_id=1, replica_groups=mesh['y'=4,'x'=4,'zh'=2,'core'=2,'row'=4] {'y','x','core'}, dimensions={0} | all-to-all | bytes 1572864 | tf_op jit(solution)/shard_map/cond/branch_4_fun/all_to_all | solution.py:352
  35.3 1.2 %collective-permute-start.4 = (f32[12,2,3,8,128]{4,3,2,1,0:T(8,128)S(1)}, f32[12,2,3,8,128]{4,3,2,1,0:T(8,128)S(1)}, u32[]{:S(2)}, u32[]{:S(2)}) collective-permute-start(f32[12,2,3,8,128]{4,3,2,1,0:T(8,128)S(1)} %outgoing.18), channel_id=1, source_target_pairs={{0,8},{8,0},{1,9},{9,1},{2,10},{10,2},{3,11},{11,3},{4,12},{12,4},... | collective-permute-start | bytes 884744 | tf_op jit(solution)/shard_map/cond/branch_4_fun/ppermute | solution.py:361
  36.5 17.5 %collective-permute-done.4.crossed_ref = f32[12,2,3,8,128]{4,3,2,1,0:T(8,128)S(1)} collective-permute-done((f32[12,2,3,8,128]{4,3,2,1,0:T(8,128)S(1)}, f32[12,2,3,8,128]{4,3,2,1,0:T(8,128)S(1)}, u32[]{:S(2)}, u32[]{:S(2)}) %collective-permute-start.4) | collective-permute-done | bytes 294944 | tf_op jit(solution)/shard_map/cond/branch_4_fun/ppermute | solution.py:361
  54.0 0.1 slots.18
  54.4 17.9 %all_to_all.75.tiles_ref = f32[32,2,3,8,128]{4,3,2,1,0:T(8,128)S(1)} all-to-all(f32[32,2,3,8,128]{4,3,2,1,0:T(8,128)S(1)} %get-tuple-element.114), channel_id=1, replica_groups=mesh['y'=4,'x'=4,'zh'=2,'core'=2,'row'=4] {'y','x','core'}, dimensions={0} | all-to-all | bytes 1572864 | tf_op jit(solution)/shard_map/all_to_all | solution.py:398
  72.4 0.9 %place.1 = f32[3,1,16,4096]{3,2,1,0:T(8,128)} custom-call(f32[32,2,3,8,128]{4,3,2,1,0:T(8,128)S(1)} %all_to_all.75.tiles_ref), custom_call_target="tpu_custom_call" | custom-call | flops 83886080 | bytes 2097152 | tf_op jit(solution)/shard_map/place/pallas_call | solution.py:373
  (1 shorter events, 0.0 us)
Async XLA Ops:
  0.0 7.5 %copy-start.1 = (f32[16,4096]{1,0:T(8,128)S(1)}, f32[16,4096]{1,0:T(8,128)}, u32[]{:S(2)}) copy-start(f32[16,4096]{1,0:T(8,128)} %ground_ref.3) | copy-start | bytes 786436
  0.0 7.5 %copy-start = (f32[3,1,16,4096]{3,2,1,0:T(8,128)S(1)}, f32[3,1,16,4096]{3,2,1,0:T(8,128)}, u32[]{:S(2)}) copy-start(f32[3,1,16,4096]{3,2,1,0:T(8,128)} %state_ref.3) | copy-start | bytes 2359300
  1.0 9.0 %collective-permute-start.15 = (f32[4,1,4096]{2,1,0:T(1,128)S(1)}, f32[4,1,4096]{2,1,0:T(1,128)S(1)}, u32[]{:S(2)}, u32[]{:S(2)}) collective-permute-start(f32[4,1,4096]{2,1,0:T(1,128)S(1)} %get-tuple-element.110), channel_id=1, source_target_pairs={{1,0},{2,1},{3,2},{8,3},{9,8},{10,9},{11,10},{0,11},{5,4},{6,5},{7... | collective-permute-start | bytes 196616 | tf_op jit(solution)/shard_map/ppermute | solution.py:332
  7.5 4.3 %collective-permute-start.14 = (f32[4,1,4096]{2,1,0:T(1,128)S(1)}, f32[4,1,4096]{2,1,0:T(1,128)S(1)}, u32[]{:S(2)}, u32[]{:S(2)}) collective-permute-start(f32[4,1,4096]{2,1,0:T(1,128)S(1)} %get-tuple-element.111), channel_id=1, source_target_pairs={{0,1},{1,2},{2,3},{3,8},{8,9},{9,10},{10,11},{11,0},{4,5},{5,6},{6... | collective-permute-start | bytes 196616 | tf_op jit(solution)/shard_map/ppermute | solution.py:331
  35.3 18.7 %collective-permute-start.4 = (f32[12,2,3,8,128]{4,3,2,1,0:T(8,128)S(1)}, f32[12,2,3,8,128]{4,3,2,1,0:T(8,128)S(1)}, u32[]{:S(2)}, u32[]{:S(2)}) collective-permute-start(f32[12,2,3,8,128]{4,3,2,1,0:T(8,128)S(1)} %outgoing.18), channel_id=1, source_target_pairs={{0,8},{8,0},{1,9},{9,1},{2,10},{10,2},{3,11},{11,3},{4,12},{12,4},... | collective-permute-start | bytes 884744 | tf_op jit(solution)/shard_map/cond/branch_4_fun/ppermute | solution.py:361
where the time goes:
time: 73.1 us; the launch traced here: 73.5 us
  blocking collectives  41.1 us (56%)
  waiting for transfers between devices  19.3 us (26%)
  starting transfers between devices  7.73 us (11%)
  Pallas kernels  4.82 us (7%)
    all_to_all x1, blocking collectives, blocks_for_slots(): held = lax.all_to_all(block, PLANE, split_axis=0, concat_axis=0, tiled=True)  23.2 us
    all_to_all x1, blocking collectives, on_device(): lax.all_to_all(chosen, PLANE, split_axis=0, concat_axis=0, tiled=True)  17.9 us
    ppermute x1, waiting for transfers between devices, blocks_for_slots(): crossed = lax.ppermute(outgoing, 'zh', SWAP)  17.5 us
    ppermute x1, starting transfers between devices, stepped_tiles(): low = lax.ppermute(first, COLUMN, backward)  6.48 us
    pallas_call x1, Pallas kernels, partial_step(): pl.pallas_call(functools.partial(step_kernel, unroll=unroll, tail=tail, s...  2.54 us
    ppermute x1, waiting for transfers between devices, stepped_tiles(): top = lax.ppermute(last, COLUMN, forward)  1.76 us
  transfers between devices with their start and end apart: 3, of which 2 were waited for; matrix products, arithmetic and copies ran while one was open for 0% of the time, Pallas kernels for 3%

commit v1 on v0

--- a/solution.py
+++ b/solution.py
@@ -243,18 +243,15 @@
         out_ref[slot] = jnp.where(code < held, near, far)
 
 
-def place_kernel(tiles_ref, out_hbm, rows_ref, sems):
-    tiles, tops, parts = tiles_ref.shape[:3]
-    copies = []
-    for part in range(parts):
-        for top in range(tops):
-            at = pl.ds(top * SUBLANES, SUBLANES)
-            for tile in range(tiles):
-                rows_ref[part, at, tile * LANES : (tile + 1) * LANES] = tiles_ref[tile, top, part]
-            copies.append(
-                pltpu.make_async_copy(rows_ref.at[part, at], out_hbm.at[part, 0, at], sems.at[part, top])
-            )
-            copies[-1].start()
+def place_kernel(tiles_ref, out_hbm, sems):
+    tops, parts = tiles_ref.shape[1:3]
+    copies = [
+        pltpu.make_async_copy(tiles_ref.at[:, top, part], out_hbm.at[part, top], sems.at[part, top])
+        for part in range(parts)
+        for top in range(tops)
+    ]
+    for copy in copies:
+        copy.start()
     for copy in copies:
         copy.wait()
 
@@ -370,18 +367,17 @@
 
 
 def placed_strip(block, rows, width):
-    return pl.pallas_call(
+    tiles, tops = block.shape[:2]
+    placed = pl.pallas_call(
         place_kernel,
-        out_shape=jax.ShapeDtypeStruct((3, 1, rows, width), jnp.float32),
+        out_shape=jax.ShapeDtypeStruct((3, tops, tiles, SUBLANES, LANES), jnp.float32),
         in_specs=whole(1),
         out_specs=HBM,
-        scratch_shapes=[
-            pltpu.VMEM((3, rows, width), jnp.float32),
-            pltpu.SemaphoreType.DMA((3, rows // SUBLANES)),
-        ],
+        scratch_shapes=[pltpu.SemaphoreType.DMA((3, tops))],
         name="place",
         **params(2 << 20),
     )(block)
+    return placed.transpose(0, 1, 3, 2, 4).reshape(3, 1, rows, width)
 
 
 PLANE = ("y", "x", "core")

time: 73.1 us -> 73.1 us (level); the launches traced: 73.5 us -> 72.4 us
  waiting for transfers between devices: 19.3 us -> 18.2 us
    ppermute x1, waiting for transfers between devices: 17.5 us -> 16.4 us  [blocks_for_slots(): crossed = lax.ppermute(outgoing, 'zh', SWAP)]
  transfers between devices with their start and end apart: 3 -> 3, of which waited for: 2 -> 2; matrix products, arithmetic and copies ran while one was open for 0% -> 0% of each run, Pallas kernels for 3% -> 4%
where the time goes in v1:
time: 73.1 us; the launch traced here: 72.4 us
  blocking collectives  41.1 us (56%)
  waiting for transfers between devices  18.2 us (25%)
  starting transfers between devices  7.73 us (11%)
  Pallas kernels  4.81 us (7%)
    all_to_all x1, blocking collectives, blocks_for_slots(): held = lax.all_to_all(block, PLANE, split_axis=0, concat_axis=0, tiled=True)  23.2 us
    all_to_all x1, blocking collectives, on_device(): lax.all_to_all(chosen, PLANE, split_axis=0, concat_axis=0, tiled=True)  17.9 us
    ppermute x1, waiting for transfers between devices, blocks_for_slots(): crossed = lax.ppermute(outgoing, 'zh', SWAP)  16.4 us
    ppermute x1, starting transfers between devices, stepped_tiles(): low = lax.ppermute(first, COLUMN, backward)  6.48 us
    pallas_call x1, Pallas kernels, partial_step(): pl.pallas_call(functools.partial(step_kernel, unroll=unroll, tail=tail, s...  2.54 us
    ppermute x1, waiting for transfers between devices, stepped_tiles(): top = lax.ppermute(last, COLUMN, forward)  1.76 us
  transfers between devices with their start and end apart: 3, of which 2 were waited for; matrix products, arithmetic and copies ran while one was open for 0% of the time, Pallas kernels for 4%

profile of v1, /device:TPU:1, one launch (start us, length us, event | category | flops | bytes accessed | tf_op | source)
XLA Modules:
  0.0 72.4 jit_solution(14684386313189411729)
XLA Ops:
  0.0 0.0 copy-start.1
  0.0 0.0 copy-start
  0.0 1.0 %pack.1 = (f32[4,1,4096]{2,1,0:T(1,128)S(1)}, f32[4,1,4096]{2,1,0:T(1,128)S(1)}) custom-call(f32[3,1,16,4096]{3,2,1,0:T(8,128)} %state_ref.3, f32[16,4096]{1,0:T(8,128)} %ground_ref.3), custom_call_target="tpu_custom_call" | custom-call | flops 10485760 | bytes 262144 | tf_op jit(solution)/shard_map/pack/pallas_call | solution.py:280
  1.0 6.5 %collective-permute-start.15 = (f32[4,1,4096]{2,1,0:T(1,128)S(1)}, f32[4,1,4096]{2,1,0:T(1,128)S(1)}, u32[]{:S(2)}, u32[]{:S(2)}) collective-permute-start(f32[4,1,4096]{2,1,0:T(1,128)S(1)} %get-tuple-element.110), channel_id=1, source_target_pairs={{1,0},{2,1},{3,2},{8,3},{9,8},{10,9},{11,10},{0,11},{5,4},{6,5},{7... | collective-permute-start | bytes 196616 | tf_op jit(solution)/shard_map/ppermute | solution.py:329
  7.5 0.0 collective-permute-start.14
  7.5 0.0 copy-done.1
  7.5 0.0 copy-done
  7.5 2.5 %step.1 = (f32[32,2,3,8,128]{4,3,2,1,0:T(8,128)S(1)}, s32[2,64]{1,0:T(2,128)S(4)}, s32[1]{0:T(128)S(4)}) custom-call(s32[1]{0:T(128)} %bitcast.zh_ref, f32[3,1,16,4096]{3,2,1,0:T(8,128)S(1)} %copy-done, f32[16,4096]{1,0:T(8,128)S(1)} %copy-done.1, f32[1,16,4096]{2,1,0:T(8,128)} %rain_hbm.1, s32[1,64]{1,0:T(1,128)} %bitcast.16, s32[1,64]{1,0:T(1,128)} %bitcast.17), custom_call_target="tpu_custom_call" | custom-call | flops 335544320 | bytes 8388608 | tf_op jit(solution)/shard_map/step/pallas_call | solution.py:299
  10.0 0.0 collective-permute-done.15
  10.0 1.8 %collective-permute-done.14 = f32[4,1,4096]{2,1,0:T(1,128)S(1)} collective-permute-done((f32[4,1,4096]{2,1,0:T(1,128)S(1)}, f32[4,1,4096]{2,1,0:T(1,128)S(1)}, u32[]{:S(2)}, u32[]{:S(2)}) %collective-permute-start.14) | collective-permute-done | bytes 65568 | tf_op jit(solution)/shard_map/ppermute | solution.py:328
  11.8 0.2 edges.1
  12.0 41.4 %conditional.1 = (f32[32,2,3,8,128]{4,3,2,1,0:T(8,128)S(1)}) conditional(s32[]{:T(128)} %bitcast.3, (f32[32,2,3,8,128]{4,3,2,1,0:T(8,128)S(1)}, s32[2,64]{1,0:T(2,128)S(4)}) %tuple.47, (f32[32,2,3,8,128]{4,3,2,1,0:T(8,128)S(1)}, s32[2,64]{1,0:T(2,128)S(4)}) %tuple.47, (f32[32,2,3,8,128]{4,3,2,1,0:T(8,128)S(1)}, ...), branch_computations={%region_0.0_spmd, %region_1.0_spmd, %region_2.0_spmd, %region_3.0_... | conditional | flops 125829120 | bytes 7864368 | solution.py:393
  12.1 23.2 %all_to_all.64.held_ref = f32[32,2,3,8,128]{4,3,2,1,0:T(8,128)S(1)} all-to-all(f32[32,2,3,8,128]{4,3,2,1,0:T(8,128)S(1)} %get-tuple-element.78), channel_id=1, replica_groups=mesh['y'=4,'x'=4,'zh'=2,'core'=2,'row'=4] {'y','x','core'}, dimensions={0} | all-to-all | bytes 1572864 | tf_op jit(solution)/shard_map/cond/branch_3_fun/all_to_all | solution.py:349
  35.3 1.2 %collective-permute-start.3 = (f32[11,2,3,8,128]{4,3,2,1,0:T(8,128)S(1)}, f32[11,2,3,8,128]{4,3,2,1,0:T(8,128)S(1)}, u32[]{:S(2)}, u32[]{:S(2)}) collective-permute-start(f32[11,2,3,8,128]{4,3,2,1,0:T(8,128)S(1)} %outgoing.17), channel_id=1, source_target_pairs={{0,8},{8,0},{1,9},{9,1},{2,10},{10,2},{3,11},{11,3},{4,12},{12,4},... | collective-permute-start | bytes 811016 | tf_op jit(solution)/shard_map/cond/branch_3_fun/ppermute | solution.py:358
  36.5 16.4 %collective-permute-done.3.crossed_ref = f32[11,2,3,8,128]{4,3,2,1,0:T(8,128)S(1)} collective-permute-done((f32[11,2,3,8,128]{4,3,2,1,0:T(8,128)S(1)}, f32[11,2,3,8,128]{4,3,2,1,0:T(8,128)S(1)}, u32[]{:S(2)}, u32[]{:S(2)}) %collective-permute-start.3) | collective-permute-done | bytes 270368 | tf_op jit(solution)/shard_map/cond/branch_3_fun/ppermute | solution.py:358
  53.0 0.1 slots.17
  53.4 17.9 %all_to_all.75.tiles_ref = f32[32,2,3,8,128]{4,3,2,1,0:T(8,128)S(1)} all-to-all(f32[32,2,3,8,128]{4,3,2,1,0:T(8,128)S(1)} %get-tuple-element.114), channel_id=1, replica_groups=mesh['y'=4,'x'=4,'zh'=2,'core'=2,'row'=4] {'y','x','core'}, dimensions={0} | all-to-all | bytes 1572864 | tf_op jit(solution)/shard_map/all_to_all | solution.py:394
  71.3 0.9 %place.1 = f32[3,2,32,8,128]{4,3,2,1,0:T(8,128)} custom-call(f32[32,2,3,8,128]{4,3,2,1,0:T(8,128)S(1)} %all_to_all.75.tiles_ref), custom_call_target="tpu_custom_call" | custom-call | flops 83886080 | bytes 2097152 | tf_op jit(solution)/shard_map/place/pallas_call | solution.py:371
  (1 shorter events, 0.0 us)
Async XLA Ops:
  0.0 7.5 %copy-start.1 = (f32[16,4096]{1,0:T(8,128)S(1)}, f32[16,4096]{1,0:T(8,128)}, u32[]{:S(2)}) copy-start(f32[16,4096]{1,0:T(8,128)} %ground_ref.3) | copy-start | bytes 786436
  0.0 7.5 %copy-start = (f32[3,1,16,4096]{3,2,1,0:T(8,128)S(1)}, f32[3,1,16,4096]{3,2,1,0:T(8,128)}, u32[]{:S(2)}) copy-start(f32[3,1,16,4096]{3,2,1,0:T(8,128)} %state_ref.3) | copy-start | bytes 2359300
  1.0 9.0 %collective-permute-start.15 = (f32[4,1,4096]{2,1,0:T(1,128)S(1)}, f32[4,1,4096]{2,1,0:T(1,128)S(1)}, u32[]{:S(2)}, u32[]{:S(2)}) collective-permute-start(f32[4,1,4096]{2,1,0:T(1,128)S(1)} %get-tuple-element.110), channel_id=1, source_target_pairs={{1,0},{2,1},{3,2},{8,3},{9,8},{10,9},{11,10},{0,11},{5,4},{6,5},{7... | collective-permute-start | bytes 196616 | tf_op jit(solution)/shard_map/ppermute | solution.py:329
  7.5 4.3 %collective-permute-start.14 = (f32[4,1,4096]{2,1,0:T(1,128)S(1)}, f32[4,1,4096]{2,1,0:T(1,128)S(1)}, u32[]{:S(2)}, u32[]{:S(2)}) collective-permute-start(f32[4,1,4096]{2,1,0:T(1,128)S(1)} %get-tuple-element.111), channel_id=1, source_target_pairs={{0,1},{1,2},{2,3},{3,8},{8,9},{9,10},{10,11},{11,0},{4,5},{5,6},{6... | collective-permute-start | bytes 196616 | tf_op jit(solution)/shard_map/ppermute | solution.py:328
  35.3 17.7 %collective-permute-start.3 = (f32[11,2,3,8,128]{4,3,2,1,0:T(8,128)S(1)}, f32[11,2,3,8,128]{4,3,2,1,0:T(8,128)S(1)}, u32[]{:S(2)}, u32[]{:S(2)}) collective-permute-start(f32[11,2,3,8,128]{4,3,2,1,0:T(8,128)S(1)} %outgoing.17), channel_id=1, source_target_pairs={{0,8},{8,0},{1,9},{9,1},{2,10},{10,2},{3,11},{11,3},{4,12},{12,4},... | collective-permute-start | bytes 811016 | tf_op jit(solution)/shard_map/cond/branch_3_fun/ppermute | solution.py:358

commit v2 on v1

--- a/solution.py
+++ b/solution.py
@@ -47,13 +47,11 @@
 
 
 def pack_kernel(state_ref, ground_ref, first_ref, last_ref, sems):
-    rows = ground_ref.shape[0]
+    tops = ground_ref.shape[0]
     copies = []
-    for side, (row, out_ref) in enumerate(((rows - 1, last_ref), (0, first_ref))):
-        at = pl.ds(row, 1)
-        for part in range(3):
-            copies.append(pltpu.make_async_copy(state_ref.at[part, 0, at], out_ref.at[part], sems.at[side, part]))
-        copies.append(pltpu.make_async_copy(ground_ref.at[at], out_ref.at[3], sems.at[side, 3]))
+    for side, (top, row, out_ref) in enumerate(((tops - 1, SUBLANES - 1, last_ref), (0, 0, first_ref))):
+        copies.append(pltpu.make_async_copy(state_ref.at[:, top, :, row], out_ref.at[0:3], sems.at[side, 0]))
+        copies.append(pltpu.make_async_copy(ground_ref.at[top, :, row], out_ref.at[3], sems.at[side, 1]))
     for copy in copies:
         copy.start()
     for copy in copies:
@@ -276,13 +274,16 @@
 
 def packed_edges(state, ground):
     rows, width = ground.shape
-    shape = pltpu.VMEM((4, 1, width), jnp.float32)
+    tops, tiles = rows // SUBLANES, width // LANES
+    shape = pltpu.VMEM((4, tiles, LANES), jnp.float32)
+    state = state.reshape(3, tops, SUBLANES, tiles, LANES).transpose(0, 1, 3, 2, 4)
+    ground = ground.reshape(tops, SUBLANES, tiles, LANES).transpose(0, 2, 1, 3)
     return pl.pallas_call(
         pack_kernel,
         out_shape=(shape, shape),
         in_specs=[HBM, HBM],
         out_specs=whole(2),
-        scratch_shapes=[pltpu.SemaphoreType.DMA((2, 4))],
+        scratch_shapes=[pltpu.SemaphoreType.DMA((2, 2))],
         name="pack",
         **params(1 << 18),
     )(*in_hbm(state, ground))

time: 73.1 us -> 76.4 us (1.045)
  waiting for transfers between devices: 18.2 us -> 21.4 us
    ppermute x1, waiting for transfers between devices: 16.4 us -> 19.6 us  [blocks_for_slots(): crossed = lax.ppermute(outgoing, 'zh', SWAP)]
  transfers between devices with their start and end apart: 3 -> 3, of which waited for: 2 -> 2; matrix products, arithmetic and copies ran while one was open for 0% -> 0% of each run, Pallas kernels for 4% -> 3%
where the time goes in v2:
time: 76.4 us; the launch traced here: 75.6 us
  blocking collectives  41.1 us (54%)
  waiting for transfers between devices  21.4 us (28%)
  starting transfers between devices  7.73 us (10%)
  Pallas kernels  4.8 us (6%)
    all_to_all x1, blocking collectives, blocks_for_slots(): held = lax.all_to_all(block, PLANE, split_axis=0, concat_axis=0, tiled=True)  23.2 us
    ppermute x1, waiting for transfers between devices, blocks_for_slots(): crossed = lax.ppermute(outgoing, 'zh', SWAP)  19.6 us
    all_to_all x1, blocking collectives, on_device(): lax.all_to_all(chosen, PLANE, split_axis=0, concat_axis=0, tiled=True)  17.9 us
    ppermute x1, starting transfers between devices, stepped_tiles(): low = lax.ppermute(first, COLUMN, backward)  6.48 us
    pallas_call x1, Pallas kernels, partial_step(): pl.pallas_call(functools.partial(step_kernel, unroll=unroll, tail=tail, s...  2.54 us
    ppermute x1, waiting for transfers between devices, stepped_tiles(): top = lax.ppermute(last, COLUMN, forward)  1.76 us
  transfers between devices with their start and end apart: 3, of which 2 were waited for; matrix products, arithmetic and copies ran while one was open for 0% of the time, Pallas kernels for 3%

profile of v2, /device:TPU:1, one launch (start us, length us, event | category | flops | bytes accessed | tf_op | source)
XLA Modules:
  0.0 75.6 jit_solution(11320254860161148758)
XLA Ops:
  0.0 0.0 copy-start
  0.0 0.0 copy-start.1
  0.0 1.0 %pack.1 = (f32[4,32,128]{2,1,0:T(8,128)S(1)}, f32[4,32,128]{2,1,0:T(8,128)S(1)}) custom-call(f32[3,2,32,8,128]{4,3,2,1,0:T(8,128)} %bitcast.14, f32[2,32,8,128]{3,2,1,0:T(8,128)} %bitcast.15), custom_call_target="tpu_custom_call" | custom-call | flops 10485760 | bytes 262144 | tf_op jit(solution)/shard_map/pack/pallas_call | solution.py:281
  1.0 6.5 %collective-permute-start.15 = (f32[4,32,128]{2,1,0:T(8,128)S(1)}, f32[4,32,128]{2,1,0:T(8,128)S(1)}, u32[]{:S(2)}, u32[]{:S(2)}) collective-permute-start(f32[4,32,128]{2,1,0:T(8,128)S(1)} %get-tuple-element.110.first_ref), channel_id=1, source_target_pairs={{1,0},{2,1},{3,2},{8,3},{9,8},{10,9},{11,10},{0,11},{5,4},{6,5},{7... | collective-permute-start | bytes 196616 | tf_op jit(solution)/shard_map/ppermute | solution.py:330
  7.5 0.0 collective-permute-start.14
  7.5 0.0 copy-done
  7.5 0.0 copy-done.1
  7.5 2.5 %step.1 = (f32[32,2,3,8,128]{4,3,2,1,0:T(8,128)S(1)}, s32[2,64]{1,0:T(2,128)S(4)}, s32[1]{0:T(128)S(4)}) custom-call(s32[1]{0:T(128)} %bitcast.zh_ref, f32[3,1,16,4096]{3,2,1,0:T(8,128)S(1)} %copy-done, f32[16,4096]{1,0:T(8,128)S(1)} %copy-done.1, f32[1,16,4096]{2,1,0:T(8,128)} %rain_hbm.1, s32[1,64]{1,0:T(1,128)} %bitcast.16, s32[1,64]{1,0:T(1,128)} %bitcast.17), custom_call_target="tpu_custom_call" | custom-call | flops 335544320 | bytes 8388608 | tf_op jit(solution)/shard_map/step/pallas_call | solution.py:300
  10.0 0.0 collective-permute-done.15.low_ref
  10.0 1.8 %collective-permute-done.14.top_ref = f32[4,32,128]{2,1,0:T(8,128)S(1)} collective-permute-done((f32[4,32,128]{2,1,0:T(8,128)S(1)}, f32[4,32,128]{2,1,0:T(8,128)S(1)}, u32[]{:S(2)}, u32[]{:S(2)}) %collective-permute-start.14) | collective-permute-done | bytes 65568 | tf_op jit(solution)/shard_map/ppermute | solution.py:329
  11.8 0.2 edges.1
  12.0 44.5 %conditional.1 = (f32[32,2,3,8,128]{4,3,2,1,0:T(8,128)S(1)}) conditional(s32[]{:T(128)} %bitcast.3, (f32[32,2,3,8,128]{4,3,2,1,0:T(8,128)S(1)}, s32[2,64]{1,0:T(2,128)S(4)}) %tuple.47, (f32[32,2,3,8,128]{4,3,2,1,0:T(8,128)S(1)}, s32[2,64]{1,0:T(2,128)S(4)}) %tuple.47, (f32[32,2,3,8,128]{4,3,2,1,0:T(8,128)S(1)}, ...), branch_computations={%region_0.0_spmd, %region_1.0_spmd, %region_2.0_spmd, %region_3.0_... | conditional | flops 125829120 | bytes 7864368 | solution.py:394
  12.1 23.2 %all_to_all.67.held_ref = f32[32,2,3,8,128]{4,3,2,1,0:T(8,128)S(1)} all-to-all(f32[32,2,3,8,128]{4,3,2,1,0:T(8,128)S(1)} %get-tuple-element.89), channel_id=1, replica_groups=mesh['y'=4,'x'=4,'zh'=2,'core'=2,'row'=4] {'y','x','core'}, dimensions={0} | all-to-all | bytes 1572864 | tf_op jit(solution)/shard_map/cond/branch_6_fun/all_to_all | solution.py:350
  35.3 1.2 %collective-permute-start.6 = (f32[14,2,3,8,128]{4,3,2,1,0:T(8,128)S(1)}, f32[14,2,3,8,128]{4,3,2,1,0:T(8,128)S(1)}, u32[]{:S(2)}, u32[]{:S(2)}) collective-permute-start(f32[14,2,3,8,128]{4,3,2,1,0:T(8,128)S(1)} %outgoing.20), channel_id=1, source_target_pairs={{0,8},{8,0},{1,9},{9,1},{2,10},{10,2},{3,11},{11,3},{4,12},{12,4},... | collective-permute-start | bytes 1032200 | tf_op jit(solution)/shard_map/cond/branch_6_fun/ppermute | solution.py:359
  36.5 19.6 %collective-permute-done.6.crossed_ref = f32[14,2,3,8,128]{4,3,2,1,0:T(8,128)S(1)} collective-permute-done((f32[14,2,3,8,128]{4,3,2,1,0:T(8,128)S(1)}, f32[14,2,3,8,128]{4,3,2,1,0:T(8,128)S(1)}, u32[]{:S(2)}, u32[]{:S(2)}) %collective-permute-start.6) | collective-permute-done | bytes 344096 | tf_op jit(solution)/shard_map/cond/branch_6_fun/ppermute | solution.py:359
  56.2 0.1 slots.20
  56.5 17.9 %all_to_all.75.tiles_ref = f32[32,2,3,8,128]{4,3,2,1,0:T(8,128)S(1)} all-to-all(f32[32,2,3,8,128]{4,3,2,1,0:T(8,128)S(1)} %get-tuple-element.114), channel_id=1, replica_groups=mesh['y'=4,'x'=4,'zh'=2,'core'=2,'row'=4] {'y','x','core'}, dimensions={0} | all-to-all | bytes 1572864 | tf_op jit(solution)/shard_map/all_to_all | solution.py:395
  74.5 0.9 %place.1 = f32[3,2,32,8,128]{4,3,2,1,0:T(8,128)} custom-call(f32[32,2,3,8,128]{4,3,2,1,0:T(8,128)S(1)} %all_to_all.75.tiles_ref), custom_call_target="tpu_custom_call" | custom-call | flops 83886080 | bytes 2097152 | tf_op jit(solution)/shard_map/place/pallas_call | solution.py:372
  (1 shorter events, 0.0 us)
Async XLA Ops:
  0.0 7.5 %copy-start = (f32[3,1,16,4096]{3,2,1,0:T(8,128)S(1)}, f32[3,1,16,4096]{3,2,1,0:T(8,128)}, u32[]{:S(2)}) copy-start(f32[3,1,16,4096]{3,2,1,0:T(8,128)} %state_ref.1) | copy-start | bytes 2359300
  0.0 7.5 %copy-start.1 = (f32[16,4096]{1,0:T(8,128)S(1)}, f32[16,4096]{1,0:T(8,128)}, u32[]{:S(2)}) copy-start(f32[16,4096]{1,0:T(8,128)} %ground_ref.1) | copy-start | bytes 786436
  1.0 9.0 %collective-permute-start.15 = (f32[4,32,128]{2,1,0:T(8,128)S(1)}, f32[4,32,128]{2,1,0:T(8,128)S(1)}, u32[]{:S(2)}, u32[]{:S(2)}) collective-permute-start(f32[4,32,128]{2,1,0:T(8,128)S(1)} %get-tuple-element.110.first_ref), channel_id=1, source_target_pairs={{1,0},{2,1},{3,2},{8,3},{9,8},{10,9},{11,10},{0,11},{5,4},{6,5},{7... | collective-permute-start | bytes 196616 | tf_op jit(solution)/shard_map/ppermute | solution.py:330
  7.5 4.3 %collective-permute-start.14 = (f32[4,32,128]{2,1,0:T(8,128)S(1)}, f32[4,32,128]{2,1,0:T(8,128)S(1)}, u32[]{:S(2)}, u32[]{:S(2)}) collective-permute-start(f32[4,32,128]{2,1,0:T(8,128)S(1)} %get-tuple-element.111.last_ref), channel_id=1, source_target_pairs={{0,1},{1,2},{2,3},{3,8},{8,9},{9,10},{10,11},{11,0},{4,5},{5,6},{6... | collective-permute-start | bytes 196616 | tf_op jit(solution)/shard_map/ppermute | solution.py:329
  35.3 20.9 %collective-permute-start.6 = (f32[14,2,3,8,128]{4,3,2,1,0:T(8,128)S(1)}, f32[14,2,3,8,128]{4,3,2,1,0:T(8,128)S(1)}, u32[]{:S(2)}, u32[]{:S(2)}) collective-permute-start(f32[14,2,3,8,128]{4,3,2,1,0:T(8,128)S(1)} %outgoing.20), channel_id=1, source_target_pairs={{0,8},{8,0},{1,9},{9,1},{2,10},{10,2},{3,11},{11,3},{4,12},{12,4},... | collective-permute-start | bytes 1032200 | tf_op jit(solution)/shard_map/cond/branch_6_fun/ppermute | solution.py:359

commit v3 on v2

--- a/solution.py
+++ b/solution.py
@@ -325,9 +325,9 @@
     first, last = packed_edges(state, ground)
     count = lax.axis_size(COLUMN)
     forward = [(i, (i + 1) % count) for i in range(count)]
-    backward = [(target, source) for source, target in forward]
+    strips_back = [(i, (i + strips - 1) % strips) for i in range(strips)]
+    low = lax.ppermute(first, "row", strips_back)
     top = lax.ppermute(last, COLUMN, forward)
-    low = lax.ppermute(first, COLUMN, backward)
     partial, plan, level = partial_step(zh, state, rain, ground, counts, slot_map, sizes)
     strip = lax.axis_index("row").astype(jnp.int32).reshape(1)
     square = (4, tiles, LANES)

time: 76.4 us -> 75 us (0.982)
  waiting for transfers between devices: 21.4 us -> 16.7 us
  starting transfers between devices: 7.73 us -> 9.55 us
  blocking collectives: 41.1 us -> 42.1 us
    ppermute x1, waiting for transfers between devices: 19.6 us -> 14.9 us  [blocks_for_slots(): crossed = lax.ppermute(outgoing, 'zh', SWAP)]
    ppermute x1, starting transfers between devices: 1.25 us -> 4.3 us  [blocks_for_slots(): crossed = lax.ppermute(outgoing, 'zh', SWAP)]
    ppermute x1, starting transfers between devices: 6.48 us -> 5.25 us  [stepped_tiles(): low = lax.ppermute(first, 'row', strips_back)]
    all_to_all x1, blocking collectives: 17.9 us -> 18.9 us  [on_device(): lax.all_to_all(chosen, PLANE, split_axis=0, concat_axis=0, tiled=True)]
where the time goes in v3:
time: 75 us; the launch traced here: 73.7 us
  blocking collectives  42.1 us (56%)
  waiting for transfers between devices  16.7 us (22%)
  starting transfers between devices  9.55 us (13%)
  Pallas kernels  4.8 us (6%)
    all_to_all x1, blocking collectives, blocks_for_slots(): held = lax.all_to_all(block, PLANE, split_axis=0, concat_axis=0, tiled=True)  23.2 us
    all_to_all x1, blocking collectives, on_device(): lax.all_to_all(chosen, PLANE, split_axis=0, concat_axis=0, tiled=True)  18.9 us
    ppermute x1, waiting for transfers between devices, blocks_for_slots(): crossed = lax.ppermute(outgoing, 'zh', SWAP)  14.9 us
    ppermute x1, starting transfers between devices, stepped_tiles(): low = lax.ppermute(first, 'row', strips_back)  5.25 us
    ppermute x1, starting transfers between devices, blocks_for_slots(): crossed = lax.ppermute(outgoing, 'zh', SWAP)  4.3 us
    pallas_call x1, Pallas kernels, partial_step(): pl.pallas_call(functools.partial(step_kernel, unroll=unroll, tail=tail, s...  2.54 us
    ppermute x1, waiting for transfers between devices, stepped_tiles(): top = lax.ppermute(last, COLUMN, forward)  1.76 us
  transfers between devices with their start and end apart: 3, of which 2 were waited for; matrix products, arithmetic and copies ran while one was open for 0% of the time, Pallas kernels for 3%

profile of v3, /device:TPU:1, one launch (start us, length us, event | category | flops | bytes accessed | tf_op | source)
XLA Modules:
  0.0 73.7 jit_solution(14028548250749588679)
XLA Ops:
  0.0 0.0 copy-start
  0.0 0.0 copy-start.1
  0.0 1.0 %pack.1 = (f32[4,32,128]{2,1,0:T(8,128)S(1)}, f32[4,32,128]{2,1,0:T(8,128)S(1)}) custom-call(f32[3,2,32,8,128]{4,3,2,1,0:T(8,128)} %bitcast.14, f32[2,32,8,128]{3,2,1,0:T(8,128)} %bitcast.15), custom_call_target="tpu_custom_call" | custom-call | flops 10485760 | bytes 262144 | tf_op jit(solution)/shard_map/pack/pallas_call | solution.py:281
  1.0 5.3 %collective-permute-start.15 = (f32[4,32,128]{2,1,0:T(8,128)S(1)}, f32[4,32,128]{2,1,0:T(8,128)S(1)}, u32[]{:S(2)}, u32[]{:S(2)}) collective-permute-start(f32[4,32,128]{2,1,0:T(8,128)S(1)} %get-tuple-element.110.first_ref), channel_id=1, source_target_pairs={{0,3},{1,0},{2,1},{3,2},{4,7},{5,4},{6,5},{7,6},{8,11},{9,8},{10,9... | collective-permute-start | bytes 196616 | tf_op jit(solution)/shard_map/ppermute | solution.py:329
  6.2 0.0 collective-permute-start.14
  6.2 0.0 copy-done
  6.2 0.0 copy-done.1
  6.2 2.5 %step.1 = (f32[32,2,3,8,128]{4,3,2,1,0:T(8,128)S(1)}, s32[2,64]{1,0:T(2,128)S(4)}, s32[1]{0:T(128)S(4)}) custom-call(s32[1]{0:T(128)} %bitcast.zh_ref, f32[3,1,16,4096]{3,2,1,0:T(8,128)S(1)} %copy-done, f32[16,4096]{1,0:T(8,128)S(1)} %copy-done.1, f32[1,16,4096]{2,1,0:T(8,128)} %rain_hbm.1, s32[1,64]{1,0:T(1,128)} %bitcast.16, s32[1,64]{1,0:T(1,128)} %bitcast.17), custom_call_target="tpu_custom_call" | custom-call | flops 335544320 | bytes 8388608 | tf_op jit(solution)/shard_map/step/pallas_call | solution.py:300
  8.8 0.0 collective-permute-done.15.low_ref
  8.8 1.8 %collective-permute-done.14.top_ref = f32[4,32,128]{2,1,0:T(8,128)S(1)} collective-permute-done((f32[4,32,128]{2,1,0:T(8,128)S(1)}, f32[4,32,128]{2,1,0:T(8,128)S(1)}, u32[]{:S(2)}, u32[]{:S(2)}) %collective-permute-start.14) | collective-permute-done | bytes 65568 | tf_op jit(solution)/shard_map/ppermute | solution.py:330
  10.6 0.2 edges.1
  10.8 42.9 %conditional.1 = (f32[32,2,3,8,128]{4,3,2,1,0:T(8,128)S(1)}) conditional(s32[]{:T(128)} %bitcast.3, (f32[32,2,3,8,128]{4,3,2,1,0:T(8,128)S(1)}, s32[2,64]{1,0:T(2,128)S(4)}) %tuple.47, (f32[32,2,3,8,128]{4,3,2,1,0:T(8,128)S(1)}, s32[2,64]{1,0:T(2,128)S(4)}) %tuple.47, (f32[32,2,3,8,128]{4,3,2,1,0:T(8,128)S(1)}, ...), branch_computations={%region_0.0_spmd, %region_1.0_spmd, %region_2.0_spmd, %region_3.0_... | conditional | flops 125829120 | bytes 7864368 | solution.py:394
  10.8 23.2 %all_to_all.66.held_ref = f32[32,2,3,8,128]{4,3,2,1,0:T(8,128)S(1)} all-to-all(f32[32,2,3,8,128]{4,3,2,1,0:T(8,128)S(1)} %get-tuple-element.86), channel_id=1, replica_groups=mesh['y'=4,'x'=4,'zh'=2,'core'=2,'row'=4] {'y','x','core'}, dimensions={0} | all-to-all | bytes 1572864 | tf_op jit(solution)/shard_map/cond/branch_5_fun/all_to_all | solution.py:350
  34.1 4.3 %collective-permute-start.5 = (f32[13,2,3,8,128]{4,3,2,1,0:T(8,128)S(1)}, f32[13,2,3,8,128]{4,3,2,1,0:T(8,128)S(1)}, u32[]{:S(2)}, u32[]{:S(2)}) collective-permute-start(f32[13,2,3,8,128]{4,3,2,1,0:T(8,128)S(1)} %outgoing.19), channel_id=1, source_target_pairs={{0,8},{8,0},{1,9},{9,1},{2,10},{10,2},{3,11},{11,3},{4,12},{12,4},... | collective-permute-start | bytes 958472 | tf_op jit(solution)/shard_map/cond/branch_5_fun/ppermute | solution.py:359
  38.4 14.9 %collective-permute-done.5.crossed_ref = f32[13,2,3,8,128]{4,3,2,1,0:T(8,128)S(1)} collective-permute-done((f32[13,2,3,8,128]{4,3,2,1,0:T(8,128)S(1)}, f32[13,2,3,8,128]{4,3,2,1,0:T(8,128)S(1)}, u32[]{:S(2)}, u32[]{:S(2)}) %collective-permute-start.5) | collective-permute-done | bytes 319520 | tf_op jit(solution)/shard_map/cond/branch_5_fun/ppermute | solution.py:359
  53.3 0.1 slots.19
  53.7 18.9 %all_to_all.75.tiles_ref = f32[32,2,3,8,128]{4,3,2,1,0:T(8,128)S(1)} all-to-all(f32[32,2,3,8,128]{4,3,2,1,0:T(8,128)S(1)} %get-tuple-element.114), channel_id=1, replica_groups=mesh['y'=4,'x'=4,'zh'=2,'core'=2,'row'=4] {'y','x','core'}, dimensions={0} | all-to-all | bytes 1572864 | tf_op jit(solution)/shard_map/all_to_all | solution.py:395
  72.6 0.9 %place.1 = f32[3,2,32,8,128]{4,3,2,1,0:T(8,128)} custom-call(f32[32,2,3,8,128]{4,3,2,1,0:T(8,128)S(1)} %all_to_all.75.tiles_ref), custom_call_target="tpu_custom_call" | custom-call | flops 83886080 | bytes 2097152 | tf_op jit(solution)/shard_map/place/pallas_call | solution.py:372
  (1 shorter events, 0.0 us)
Async XLA Ops:
  0.0 6.2 %copy-start = (f32[3,1,16,4096]{3,2,1,0:T(8,128)S(1)}, f32[3,1,16,4096]{3,2,1,0:T(8,128)}, u32[]{:S(2)}) copy-start(f32[3,1,16,4096]{3,2,1,0:T(8,128)} %state_ref.1) | copy-start | bytes 2359300
  0.0 6.2 %copy-start.1 = (f32[16,4096]{1,0:T(8,128)S(1)}, f32[16,4096]{1,0:T(8,128)}, u32[]{:S(2)}) copy-start(f32[16,4096]{1,0:T(8,128)} %ground_ref.1) | copy-start | bytes 786436
  1.0 7.8 %collective-permute-start.15 = (f32[4,32,128]{2,1,0:T(8,128)S(1)}, f32[4,32,128]{2,1,0:T(8,128)S(1)}, u32[]{:S(2)}, u32[]{:S(2)}) collective-permute-start(f32[4,32,128]{2,1,0:T(8,128)S(1)} %get-tuple-element.110.first_ref), channel_id=1, source_target_pairs={{0,3},{1,0},{2,1},{3,2},{4,7},{5,4},{6,5},{7,6},{8,11},{9,8},{10,9... | collective-permute-start | bytes 196616 | tf_op jit(solution)/shard_map/ppermute | solution.py:329
  6.2 4.3 %collective-permute-start.14 = (f32[4,32,128]{2,1,0:T(8,128)S(1)}, f32[4,32,128]{2,1,0:T(8,128)S(1)}, u32[]{:S(2)}, u32[]{:S(2)}) collective-permute-start(f32[4,32,128]{2,1,0:T(8,128)S(1)} %get-tuple-element.111.last_ref), channel_id=1, source_target_pairs={{0,1},{1,2},{2,3},{3,8},{8,9},{9,10},{10,11},{11,0},{4,5},{5,6},{6... | collective-permute-start | bytes 196616 | tf_op jit(solution)/shard_map/ppermute | solution.py:330
  34.1 19.2 %collective-permute-start.5 = (f32[13,2,3,8,128]{4,3,2,1,0:T(8,128)S(1)}, f32[13,2,3,8,128]{4,3,2,1,0:T(8,128)S(1)}, u32[]{:S(2)}, u32[]{:S(2)}) collective-permute-start(f32[13,2,3,8,128]{4,3,2,1,0:T(8,128)S(1)} %outgoing.19), channel_id=1, source_target_pairs={{0,8},{8,0},{1,9},{9,1},{2,10},{10,2},{3,11},{11,3},{4,12},{12,4},... | collective-permute-start | bytes 958472 | tf_op jit(solution)/shard_map/cond/branch_5_fun/ppermute | solution.py:359

commit v4 on v2

--- a/solution.py
+++ b/solution.py
@@ -191,7 +191,7 @@
     to_scalars.wait()
 
 
-def edge_kernel(strip_ref, first_ref, last_ref, top_ref, low_ref, part_ref, out_ref, top_sc, low_sc, *, strips):
+def edge_kernel(strip_ref, last_ref, first_ref, low_ref, top_ref, part_ref, out_ref, top_sc, low_sc, *, strips):
     strip = strip_ref[0]
 
     def fluxes(inside, outside, at_wall, upward):
@@ -339,7 +339,7 @@
         scratch_shapes=[pltpu.VMEM((3, tiles, LANES), jnp.float32)] * 2,
         name="edges",
         **params(1 << 20),
-    )(strip, first.reshape(square), last.reshape(square), top.reshape(square), low.reshape(square), partial)
+    )(strip, last.reshape(square), first.reshape(square), low.reshape(square), top.reshape(square), partial)
     return block, plan, level
 
 

time: 76.4 us -> 70.6 us (0.924)
  the two profiles are of different devices: /device:TPU:1 before, /device:TPU:97 now
where the time goes in v4:
time: 70.6 us; the launch traced here: 71.4 us
  blocking collectives  41.4 us (59%)
  waiting for transfers between devices  20.5 us (29%)
  Pallas kernels  4.8 us (7%)
  starting transfers between devices  4.19 us (6%)
    all_to_all x1, blocking collectives, blocks_for_slots(): held = lax.all_to_all(block, PLANE, split_axis=0, concat_axis=0, tiled=True)  23.2 us
    ppermute x1, waiting for transfers between devices, blocks_for_slots(): crossed = lax.ppermute(outgoing, 'zh', SWAP)  18.7 us
    all_to_all x1, blocking collectives, on_device(): lax.all_to_all(chosen, PLANE, split_axis=0, concat_axis=0, tiled=True)  18.2 us
    ppermute x1, starting transfers between devices, stepped_tiles(): top = lax.ppermute(last, COLUMN, forward)  2.93 us
    pallas_call x1, Pallas kernels, partial_step(): pl.pallas_call(functools.partial(step_kernel, unroll=unroll, tail=tail, s...  2.54 us
    ppermute x1, waiting for transfers between devices, stepped_tiles(): low = lax.ppermute(first, COLUMN, backward)  1.76 us
  transfers between devices with their start and end apart: 3, of which 2 were waited for; matrix products, arithmetic and copies ran while one was open for 0% of the time, Pallas kernels for 4%

profile of v4, /device:TPU:97, one launch (start us, length us, event | category | flops | bytes accessed | tf_op | source)
XLA Modules:
  0.0 71.4 jit_solution(3372966610040167826)
XLA Ops:
  0.0 0.0 copy-start
  0.0 0.0 copy-start.1
  0.0 1.0 %pack.1 = (f32[4,32,128]{2,1,0:T(8,128)S(1)}, f32[4,32,128]{2,1,0:T(8,128)S(1)}) custom-call(f32[3,2,32,8,128]{4,3,2,1,0:T(8,128)} %bitcast.14, f32[2,32,8,128]{3,2,1,0:T(8,128)} %bitcast.15), custom_call_target="tpu_custom_call" | custom-call | flops 10485760 | bytes 262144 | tf_op jit(solution)/shard_map/pack/pallas_call | solution.py:281
  1.0 2.9 %collective-permute-start.15 = (f32[4,32,128]{2,1,0:T(8,128)S(1)}, f32[4,32,128]{2,1,0:T(8,128)S(1)}, u32[]{:S(2)}, u32[]{:S(2)}) collective-permute-start(f32[4,32,128]{2,1,0:T(8,128)S(1)} %get-tuple-element.110.last_ref), channel_id=1, source_target_pairs={{0,1},{1,2},{2,3},{3,8},{8,9},{9,10},{10,11},{11,0},{4,5},{5,6},{6... | collective-permute-start | bytes 196616 | tf_op jit(solution)/shard_map/ppermute | solution.py:329
  3.9 0.0 collective-permute-start.14
  3.9 0.0 copy-done
  3.9 0.0 copy-done.1
  3.9 2.5 %step.1 = (f32[32,2,3,8,128]{4,3,2,1,0:T(8,128)S(1)}, s32[2,64]{1,0:T(2,128)S(4)}, s32[1]{0:T(128)S(4)}) custom-call(s32[1]{0:T(128)} %bitcast.zh_ref, f32[3,1,16,4096]{3,2,1,0:T(8,128)S(1)} %copy-done, f32[16,4096]{1,0:T(8,128)S(1)} %copy-done.1, f32[1,16,4096]{2,1,0:T(8,128)} %rain_hbm.1, s32[1,64]{1,0:T(1,128)} %bitcast.16, s32[1,64]{1,0:T(1,128)} %bitcast.17), custom_call_target="tpu_custom_call" | custom-call | flops 335544320 | bytes 8388608 | tf_op jit(solution)/shard_map/step/pallas_call | solution.py:300
  6.5 0.0 collective-permute-done.15.top_ref
  6.5 1.8 %collective-permute-done.14.low_ref = f32[4,32,128]{2,1,0:T(8,128)S(1)} collective-permute-done((f32[4,32,128]{2,1,0:T(8,128)S(1)}, f32[4,32,128]{2,1,0:T(8,128)S(1)}, u32[]{:S(2)}, u32[]{:S(2)}) %collective-permute-start.14) | collective-permute-done | bytes 65568 | tf_op jit(solution)/shard_map/ppermute | solution.py:330
  8.2 0.2 edges.1
  8.4 43.7 %conditional.1 = (f32[32,2,3,8,128]{4,3,2,1,0:T(8,128)S(1)}) conditional(s32[]{:T(128)} %bitcast.3, (f32[32,2,3,8,128]{4,3,2,1,0:T(8,128)S(1)}, s32[2,64]{1,0:T(2,128)S(4)}) %tuple.47, (f32[32,2,3,8,128]{4,3,2,1,0:T(8,128)S(1)}, s32[2,64]{1,0:T(2,128)S(4)}) %tuple.47, (f32[32,2,3,8,128]{4,3,2,1,0:T(8,128)S(1)}, ...), branch_computations={%region_0.0_spmd, %region_1.0_spmd, %region_2.0_spmd, %region_3.0_... | conditional | flops 125829120 | bytes 7864368 | solution.py:394
  8.5 23.2 %all_to_all.66.held_ref = f32[32,2,3,8,128]{4,3,2,1,0:T(8,128)S(1)} all-to-all(f32[32,2,3,8,128]{4,3,2,1,0:T(8,128)S(1)} %get-tuple-element.86), channel_id=1, replica_groups=mesh['y'=4,'x'=4,'zh'=2,'core'=2,'row'=4] {'y','x','core'}, dimensions={0} | all-to-all | bytes 1572864 | tf_op jit(solution)/shard_map/cond/branch_5_fun/all_to_all | solution.py:350
  31.7 1.3 %collective-permute-start.5 = (f32[13,2,3,8,128]{4,3,2,1,0:T(8,128)S(1)}, f32[13,2,3,8,128]{4,3,2,1,0:T(8,128)S(1)}, u32[]{:S(2)}, u32[]{:S(2)}) collective-permute-start(f32[13,2,3,8,128]{4,3,2,1,0:T(8,128)S(1)} %outgoing.19), channel_id=1, source_target_pairs={{0,8},{8,0},{1,9},{9,1},{2,10},{10,2},{3,11},{11,3},{4,12},{12,4},... | collective-permute-start | bytes 958472 | tf_op jit(solution)/shard_map/cond/branch_5_fun/ppermute | solution.py:359
  33.0 18.7 %collective-permute-done.5.crossed_ref = f32[13,2,3,8,128]{4,3,2,1,0:T(8,128)S(1)} collective-permute-done((f32[13,2,3,8,128]{4,3,2,1,0:T(8,128)S(1)}, f32[13,2,3,8,128]{4,3,2,1,0:T(8,128)S(1)}, u32[]{:S(2)}, u32[]{:S(2)}) %collective-permute-start.5) | collective-permute-done | bytes 319520 | tf_op jit(solution)/shard_map/cond/branch_5_fun/ppermute | solution.py:359
  51.7 0.1 slots.19
  52.1 18.2 %all_to_all.75.tiles_ref = f32[32,2,3,8,128]{4,3,2,1,0:T(8,128)S(1)} all-to-all(f32[32,2,3,8,128]{4,3,2,1,0:T(8,128)S(1)} %get-tuple-element.114), channel_id=1, replica_groups=mesh['y'=4,'x'=4,'zh'=2,'core'=2,'row'=4] {'y','x','core'}, dimensions={0} | all-to-all | bytes 1572864 | tf_op jit(solution)/shard_map/all_to_all | solution.py:395
  70.3 0.9 %place.1 = f32[3,2,32,8,128]{4,3,2,1,0:T(8,128)} custom-call(f32[32,2,3,8,128]{4,3,2,1,0:T(8,128)S(1)} %all_to_all.75.tiles_ref), custom_call_target="tpu_custom_call" | custom-call | flops 83886080 | bytes 2097152 | tf_op jit(solution)/shard_map/place/pallas_call | solution.py:372
  (1 shorter events, 0.0 us)
Async XLA Ops:
  0.0 3.9 %copy-start = (f32[3,1,16,4096]{3,2,1,0:T(8,128)S(1)}, f32[3,1,16,4096]{3,2,1,0:T(8,128)}, u32[]{:S(2)}) copy-start(f32[3,1,16,4096]{3,2,1,0:T(8,128)} %state_ref.1) | copy-start | bytes 2359300
  0.0 3.9 %copy-start.1 = (f32[16,4096]{1,0:T(8,128)S(1)}, f32[16,4096]{1,0:T(8,128)}, u32[]{:S(2)}) copy-start(f32[16,4096]{1,0:T(8,128)} %ground_ref.1) | copy-start | bytes 786436
  1.0 5.5 %collective-permute-start.15 = (f32[4,32,128]{2,1,0:T(8,128)S(1)}, f32[4,32,128]{2,1,0:T(8,128)S(1)}, u32[]{:S(2)}, u32[]{:S(2)}) collective-permute-start(f32[4,32,128]{2,1,0:T(8,128)S(1)} %get-tuple-element.110.last_ref), channel_id=1, source_target_pairs={{0,1},{1,2},{2,3},{3,8},{8,9},{9,10},{10,11},{11,0},{4,5},{5,6},{6... | collective-permute-start | bytes 196616 | tf_op jit(solution)/shard_map/ppermute | solution.py:329
  3.9 4.3 %collective-permute-start.14 = (f32[4,32,128]{2,1,0:T(8,128)S(1)}, f32[4,32,128]{2,1,0:T(8,128)S(1)}, u32[]{:S(2)}, u32[]{:S(2)}) collective-permute-start(f32[4,32,128]{2,1,0:T(8,128)S(1)} %get-tuple-element.111.first_ref), channel_id=1, source_target_pairs={{1,0},{2,1},{3,2},{8,3},{9,8},{10,9},{11,10},{0,11},{5,4},{6,5},{7... | collective-permute-start | bytes 196616 | tf_op jit(solution)/shard_map/ppermute | solution.py:330
  31.7 20.0 %collective-permute-start.5 = (f32[13,2,3,8,128]{4,3,2,1,0:T(8,128)S(1)}, f32[13,2,3,8,128]{4,3,2,1,0:T(8,128)S(1)}, u32[]{:S(2)}, u32[]{:S(2)}) collective-permute-start(f32[13,2,3,8,128]{4,3,2,1,0:T(8,128)S(1)} %outgoing.19), channel_id=1, source_target_pairs={{0,8},{8,0},{1,9},{9,1},{2,10},{10,2},{3,11},{11,3},{4,12},{12,4},... | collective-permute-start | bytes 958472 | tf_op jit(solution)/shard_map/cond/branch_5_fun/ppermute | solution.py:359
